TPU v7x, 32 devices: a whole 2x2x4 slice. The times are simulated.
32 devices in a mesh: dp: 8 (over z, x), group: 2 (over core), mp: 2 (over y).
Axes of the slice: x: 2, y: 2, z: 4, core: 2. Of those that a mesh axis runs over, the one named last changes fastest.
Arguments:
- teacher_rows: bfloat16 [5120, 5120], P('dp', ('group', 'mp')), may hold values from -500 to 500
- teacher_gain: bfloat16 [5120], P(('group', 'mp')), may hold values from 0.099609375 to 1.8984375
- teacher_head: bfloat16 [1536, 5120], P(('group', 'mp'), 'dp'), may hold values from -3 to 3
- student_rows: bfloat16 [5120, 2048], P('dp'), may hold values from -500 to 500
- student_gain: bfloat16 [2048], replicated, may hold values from 0.099609375 to 1.8984375
- student_head: bfloat16 [1536, 2048], P(('group', 'mp'), 'dp'), may hold values from -3 to 3
- lengths: int32 [8], P('dp'), may hold values from 384 to 640, as said below
Outputs:
- head_update: bfloat16 [1536, 2048], P(('group', 'mp'), 'dp')
- row_update: bfloat16 [5120, 2048], P(('dp', 'group', 'mp'))
Inputs may be any that keep to these rules, and one draw needn't show every extreme that they name: `lengths`: the first sequence has exactly 384 tokens and the last exactly 640.
All inputs are finite; a program needn't handle non-finite values.
Results may differ from a plain program's by a relative error of at most 0.023.
Values may be sent and summed in bfloat16 or wider, within the bound.
A program may use at most 64 MiB of HBM per device.

v0:
```python
import jax
import jax.numpy as jnp
from jax import lax
from jax.sharding import PartitionSpec as P

DT = 5120
LMAX = 640


epsilon = 1e-06


def normalize(rows, gain):
    values = rows.astype(jnp.float32)
    mean_square = jnp.mean(values * values, axis=-1, keepdims=True)
    return (values * lax.rsqrt(mean_square + epsilon) * gain.astype(jnp.float32)).astype(
        jnp.bfloat16
    )


def against(rows, weights):
    return lax.dot_general(
        rows, weights, (((1,), (1,)), ((), ())), preferred_element_type=jnp.float32
    )


def body(
    teacher_rows, teacher_gain, teacher_head, student_rows, student_gain, student_head, lengths
):
    head_teacher, head_student = (
        lax.all_gather(teacher_head, "dp", axis=1, tiled=True),
        lax.all_gather(student_head, "dp", axis=1, tiled=True),
    )
    student_normed = normalize(student_rows, student_gain)
    tokens = student_rows.shape[0]
    values = teacher_rows.astype(jnp.float32)
    squares = lax.psum(jnp.sum(values * values, axis=1), ("group", "mp"))
    scale = lax.rsqrt(squares / DT + epsilon)
    teacher_normed = (values * scale[:, None] * teacher_gain.astype(jnp.float32)).astype(
        jnp.bfloat16
    )
    teacher_logits = against(
        lax.all_gather(teacher_normed, ("group", "mp"), axis=1, tiled=True), head_teacher
    )
    student_logits = against(student_normed, head_student)
    teacher_top, student_top = lax.pmax(
        (jnp.max(teacher_logits, axis=1), jnp.max(student_logits, axis=1)), ("group", "mp")
    )
    teacher_sum, student_sum = lax.psum(
        (
            jnp.sum(jnp.exp(teacher_logits - teacher_top[:, None]), axis=1),
            jnp.sum(jnp.exp(student_logits - student_top[:, None]), axis=1),
        ),
        ("group", "mp"),
    )
    teacher_lse = teacher_top + jnp.log(teacher_sum)
    student_lse = student_top + jnp.log(student_sum)
    position = jnp.arange(tokens, dtype=jnp.int32) % LMAX
    live = (position < jnp.repeat(lengths, LMAX, total_repeat_length=tokens)).astype(jnp.float32)
    teacher_prob = jnp.exp(teacher_logits - teacher_lse[:, None])
    student_prob = jnp.exp(student_logits - student_lse[:, None])
    logit_grad = (live[:, None] * (student_prob - teacher_prob)).astype(jnp.bfloat16)
    head_grad = (
        lax.psum_scatter(
            lax.dot_general(
                student_normed,
                logit_grad,
                (((0,), (0,)), ((), ())),
                preferred_element_type=jnp.float32,
            ).astype(jnp.bfloat16),
            "dp",
            scatter_dimension=0,
            tiled=True,
        )
        .astype(jnp.float32)
        .T
    )
    rows = lax.slice_in_dim(
        logit_grad,
        0,
        tokens // lax.axis_size(("group", "mp")) * lax.axis_size(("group", "mp")),
        axis=0,
    )
    row_grad = lax.psum_scatter(
        jnp.dot(rows, head_student, preferred_element_type=jnp.float32).astype(jnp.bfloat16),
        ("group", "mp"),
        scatter_dimension=0,
        tiled=True,
    ).astype(jnp.float32)
    devices = lax.axis_size(("dp", "group", "mp"))
    head_square, row_square = lax.psum(
        (jnp.sum(head_grad * head_grad), jnp.sum(row_grad * row_grad)), ("dp", "group", "mp")
    )
    head_update = head_grad * lax.rsqrt(head_square / (head_grad.size * devices) + epsilon)
    row_update = row_grad * lax.rsqrt(row_square / (row_grad.size * devices) + epsilon)
    return (head_update.astype(jnp.bfloat16), row_update.astype(jnp.bfloat16))


def solution(mesh):
    placed = (
        P("dp", ("group", "mp")),
        P(("group", "mp")),
        P(("group", "mp"), "dp"),
        P("dp", None),
        P(),
        P(("group", "mp"), "dp"),
        P("dp"),
    )
    return jax.shard_map(
        body,
        mesh=mesh,
        in_specs=placed,
        out_specs=(P(("group", "mp"), "dp"), P(("dp", "group", "mp"), None)),
        check_vma=False,
    )
```

profile of v0, /device:TPU:0, one launch (start us, length us, event | category | flops | bytes accessed | tf_op | source)
XLA Modules:
  0.0 358.7 jit_solution(17733086986654489811)
XLA Ops:
  7.2 0.7 all-gather.4.cloned.1.call-update
  8.0 0.7 all-gather.8.cloned.1.call-update
  8.7 0.7 convert_element_type.54
  9.4 1.8 fusion.3
  11.2 9.0 %psum.36 = f32[640]{0:T(1024)S(1)} all-reduce(f32[640]{0:T(1024)S(1)} %fusion.3), channel_id=1, replica_groups=mesh['dp'=8,'group'=2,'mp'=2] {'group','mp'}, use_global_device_ids=true, to_apply=%region_6.0 | all-reduce | flops 640 | bytes 5120 | tf_op jit(solution)/shard_map/psum | solution.py:37
  20.2 1.6 fusion.5
  22.6 2.3 fusion
  24.9 33.2 %all-gather.4.cloned.1.call-done = bf16[384,2048]{1,0:T(8,128)(2,1)} async-done(((bf16[384,256]{1,0:T(8,128)(2,1)}), bf16[384,2048]{1,0:T(8,128)(2,1)}) %all-gather.4.cloned.1.call-update) | async-done | bytes 1572880 | tf_op jit(solution)/shard_map/all_gather | solution.py:32
  58.1 3.7 %fusion.16 = (f32[640]{0:T(1024)S(1)}, f32[640,384]{0,1:T(8,128)S(1)}) fusion(bf16[384,2048]{1,0:T(8,128)(2,1)} %all-gather.4.cloned.1.call-done, bf16[640,2048]{1,0:T(8,128)(2,1)} %param.14, f32[2048]{0:T(1024)S(1)} %convert_element_type.50, f32[640]{0:T(1024)S(1)} %add_rsqrt_fusion.1), kind=kOutput, calls=%fused_computation.32 | convolution fusion | flops 1012120960 | bytes 5190656 | tf_op jit(solution)/shard_map/dot_general | solution.py:22
  61.8 66.5 %all-gather.8.cloned.1.call-done = bf16[384,5120]{1,0:T(8,128)(2,1)} async-done(((bf16[384,640]{1,0:T(8,128)(2,1)}), bf16[384,5120]{1,0:T(8,128)(2,1)}) %all-gather.8.cloned.1.call-update) | async-done | bytes 3932176 | tf_op jit(solution)/shard_map/all_gather | solution.py:31
  128.3 48.2 %all-gather.6.cloned.1.call-done = bf16[640,5120]{1,0:T(8,128)(2,1)} async-done(((bf16[640,1280]{1,0:T(8,128)(2,1)}), bf16[640,5120]{1,0:T(8,128)(2,1)}) %all-gather.6.cloned.1.call-update) | async-done | bytes 6553616 | tf_op jit(solution)/shard_map/all_gather | solution.py:43
  176.5 7.2 %fusion.15 = (f32[640]{0:T(1024)S(1)}, f32[640,384]{0,1:T(8,128)S(1)}) fusion(bf16[640,5120]{1,0:T(8,128)(2,1)} %all-gather.6.cloned.1.call-done, bf16[384,5120]{1,0:T(8,128)(2,1)} %all-gather.8.cloned.1.call-done), kind=kOutput, calls=%fused_computation.31 | convolution fusion | flops 2516827648 | bytes 11471360 | tf_op jit(solution)/shard_map/dot_general | solution.py:22
  183.8 6.4 %all-reduce.2 = (f32[640]{0:T(1024)S(1)}, f32[640]{0:T(1024)S(1)}) all-reduce(f32[640]{0:T(1024)S(1)} %get-tuple-element.34, f32[640]{0:T(1024)S(1)} %get-tuple-element.36), channel_id=1, replica_groups=mesh['dp'=8,'group'=2,'mp'=2] {'group','mp'}, use_global_device_ids=true, to_apply=%region_8.0 | all-reduce | flops 1280 | bytes 10240 | tf_op jit(solution)/shard_map/pmax | solution.py:46
  190.5 8.4 %all-reduce.1 = (f32[640]{0:T(1024)S(1)}, f32[640]{0:T(1024)S(1)}) all-reduce(f32[640]{0:T(1024)S(1)} %get-tuple-element.38, f32[640]{0:T(1024)S(1)} %get-tuple-element.39), channel_id=1, replica_groups=mesh['dp'=8,'group'=2,'mp'=2] {'group','mp'}, use_global_device_ids=true, to_apply=%region_10.0 | all-reduce | flops 1280 | bytes 10240 | tf_op jit(solution)/shard_map/psum | solution.py:49
  199.2 4.8 %convolution_convert_fusion.1 = bf16[2048,384]{1,0:T(8,128)(2,1)} fusion(bf16[640,384]{0,1:T(8,128)(2,1)S(1)} %multiply_convert_fusion, bf16[640,2048]{1,0:T(8,128)(2,1)} %param.14, f32[2048]{0:T(1024)S(1)} %convert_element_type.50, f32[640]{0:T(1024)S(1)} %add_rsqrt_fusion.1), kind=kOutput, calls=%fused_computation.11 | convolution fusion | flops 1012662272 | bytes 4696576 | tf_op jit(solution)/shard_map/dot_general | solution.py:65
  204.1 3.1 convolution_convert_fusion
  207.2 61.9 %reduce-scatter.3.cloned.1.call-done = bf16[256,384]{1,0:T(8,128)(2,1)} async-done(((bf16[2048,384]{1,0:T(8,128)(2,1)}), bf16[256,384]{1,0:T(8,128)(2,1)}) %reduce-scatter.3.cloned.1.call-update) | async-done | bytes 196624 | tf_op jit(solution)/shard_map/reduce_scatter | solution.py:64
  269.1 1.6 fusion.11
  270.8 34.6 %reduce-scatter.5.cloned.1.call-done = bf16[160,2048]{1,0:T(8,128)(2,1)} async-done(((bf16[640,2048]{1,0:T(8,128)(2,1)}), bf16[160,2048]{1,0:T(8,128)(2,1)}) %reduce-scatter.5.cloned.1.call-update) | async-done | bytes 655376 | tf_op jit(solution)/shard_map/reduce_scatter | solution.py:84
  305.3 2.0 fusion.6
  307.4 39.6 %all-reduce = (f32[]{:T(128)}, f32[]{:T(128)}) all-reduce(f32[]{:T(128)} %fusion.11, f32[]{:T(128)} %fusion.6), channel_id=1, replica_groups=mesh['dp'=8,'group'=2,'mp'=2] {'dp','group','mp'}, use_global_device_ids=true, to_apply=%region_13.14 | all-reduce | flops 2 | bytes 16 | tf_op jit(solution)/shard_map/psum | solution.py:91
  347.6 1.0 fusion.13
  348.6 0.8 copy.9
  350.1 2.0 fusion.7
  (22 shorter events, 0.9 us)
Async XLA Ops:
  7.2 13.0 %copy-start = (bf16[640,1280]{1,0:T(8,128)(2,1)S(1)}, bf16[640,1280]{1,0:T(8,128)(2,1)}, u32[]{:S(2)}) copy-start(bf16[640,1280]{1,0:T(8,128)(2,1)} %param.11) | copy-start | bytes 4915204
  7.2 50.9 %all-gather.4.cloned.1.call-start = ((), (), s32[]{:S(2)}) async-start(), calls=%async_computation.2 | async-start | bytes 1769472 | tf_op jit(solution)/shard_map/all_gather | solution.py:32
  7.9 120.4 %all-gather.8.cloned.1.call-start = ((), (), s32[]{:S(2)}) async-start(), calls=%async_computation.4 | async-start | bytes 4423680 | tf_op jit(solution)/shard_map/all_gather | solution.py:31
  8.7 167.9 %all-gather.6.cloned.1.call-start = ((), (), s32[]{:S(2)}) async-start(), calls=%async_computation.3 | async-start | bytes 8192000 | tf_op jit(solution)/shard_map/all_gather | solution.py:43
  11.2 10.7 %copy-start.1 = (bf16[2048]{0:T(1024)(128)(2,1)S(1)}, bf16[2048]{0:T(1024)(128)(2,1)}, u32[]{:S(2)}) copy-start(bf16[2048]{0:T(1024)(128)(2,1)} %param.15) | copy-start | bytes 12292
  21.8 247.3 %reduce-scatter.3.cloned.1.call-start = ((), (), s32[]{:S(2)}) async-start(), calls=%async_computation.5 | async-start | bytes 1769472 | tf_op jit(solution)/shard_map/reduce_scatter | solution.py:64
  199.2 4.9 %copy-start.2 = (bf16[384,2048]{1,0:T(8,128)(2,1)S(1)}, bf16[384,2048]{1,0:T(8,128)(2,1)}, u32[]{:S(2)}) copy-start(bf16[384,2048]{1,0:T(8,128)(2,1)} %all-gather.4.cloned.1.call-done) | copy-start | bytes 4718596
  204.1 101.3 %reduce-scatter.5.cloned.1.call-start = ((), (), s32[]{:S(2)}) async-start(), calls=%async_computation.6 | async-start | bytes 3276800 | tf_op jit(solution)/shard_map/reduce_scatter | solution.py:84
Sparse Core Ops, SparseCore 0:
  10.1 47.9 all-gather.3
  60.3 67.9 all-gather.7
  129.9 46.5 all-gather.5
  204.2 64.9 reduce-scatter.2
  271.7 33.5 reduce-scatter.4
where the time goes:
time: 359 us
  waiting for transfers between devices  246 us (69%)
  blocking collectives  63.4 us (18%)
  matrix products  18.8 us (5%)
  between operations  15.9 us (4%)
  other arithmetic  13.7 us (4%)
    all_gather x1, waiting for transfers between devices, body(): lax.all_gather(teacher_head, 'dp', axis=1, tiled=True)  66.5 us
    reduce_scatter x1, waiting for transfers between devices, body(): lax.psum_scatter(lax.dot_general(student_normed, logit_grad, (((0,), (0,)...  61.9 us
    all_gather x1, waiting for transfers between devices, body(): lax.all_gather(teacher_normed, ('group', 'mp'), axis=1, tiled=True)  48.2 us
    psum x1, blocking collectives, body(): lax.psum((jnp.sum(head_grad * head_grad), jnp.sum(row_grad * row_grad)),...  39.6 us
    reduce_scatter x1, waiting for transfers between devices, body(): lax.psum_scatter(jnp.dot(rows, head_student, preferred_element_type=jnp.f...  34.6 us
    all_gather x1, waiting for transfers between devices, body(): lax.all_gather(student_head, 'dp', axis=1, tiled=True)  33.2 us
    dot_general x2, matrix products, against(): lax.dot_general(rows, weights, (((1,), (1,)), ((), ())), preferred_elemen...  10.9 us
    psum x1, blocking collectives, body(): squares = lax.psum(jnp.sum(values * values, axis=1), ('group', 'mp'))  8.95 us
  transfers between devices with their start and end apart: 5, of which 5 were waited for; matrix products, arithmetic and copies ran while one was open for 4% of the time, Pallas kernels for 0%

commit v1 on v0

--- a/solution.py
+++ b/solution.py
@@ -1,6 +1,10 @@
+import functools
+
 import jax
 import jax.numpy as jnp
 from jax import lax
+from jax.experimental import pallas as pl
+from jax.experimental.pallas import tpu as pltpu
 from jax.sharding import PartitionSpec as P
 
 DT = 5120
@@ -96,6 +100,382 @@
     return (head_update.astype(jnp.bfloat16), row_update.astype(jnp.bfloat16))
 
 
+MESH = pl.DeviceIdType.MESH
+COLS = 2
+CHUNKS = 3
+
+
+def dot_nt(a, b):
+    return lax.dot_general(a, b, (((1,), (1,)), ((), ())), preferred_element_type=jnp.float32)
+
+
+def step_kernel(
+    n_dp,
+    t_rows, t_gain, t_head, s_rows, s_gain, s_head, live,
+    head_out, row_out,
+    rows_all, gain_all, ht, hs, srow, sn, tn, t_exp, s_exp, lg_t, lg,
+    stat, stat_in, hx_out, hx_in, hz_out, hz_in, h_acc,
+    rc_out, rc_in, ry_out, ry_in, r_acc, sq, sq_in, sq2, sq2_in,
+    send_sem, recv_sem, local_sem,
+):
+    n_z = n_dp // COLS
+    d, g, m = lax.axis_index("dp"), lax.axis_index("group"), lax.axis_index("mp")
+    z, x = d // COLS, d % COLS
+    px, pg, pm = 1 - x, 1 - g, 1 - m
+    me = 2 * g + m
+    voc, tf = t_head.shape
+    sf = s_head.shape[1]
+    tok, ds = s_rows.shape
+    blocks = 4
+    own = tok // blocks
+    peers = [dict(group=g, mp=pm), dict(group=pg, mp=m), dict(group=pg, mp=pm)]
+    peers_gm = [2 * g + pm, 2 * pg + m, 2 * pg + pm]
+
+    barrier = pltpu.get_barrier_semaphore()
+    for peer in peers:
+        pl.semaphore_signal(barrier, inc=1, device_id=peer, device_id_type=MESH)
+    for k in range(1, n_dp):
+        pl.semaphore_signal(
+            barrier, inc=1, device_id={"dp": (d + k) % n_dp}, device_id_type=MESH
+        )
+
+    locals_ = [
+        pltpu.make_async_copy(src, dst, local_sem.at[i])
+        for i, (src, dst) in enumerate(
+            [
+                (s_rows, srow),
+                (t_rows, rows_all.at[me]),
+                (t_head, ht.at[d]),
+                (s_head, hs.at[d]),
+                (t_gain, gain_all.at[me]),
+            ]
+        )
+    ]
+    for copy in locals_:
+        copy.start()
+    pl.semaphore_wait(barrier, 3 + n_dp - 1)
+
+    sent = []
+
+    def send(src, dst, to):
+        i = len(sent)
+        copy = pltpu.make_async_remote_copy(
+            src_ref=src, dst_ref=dst, send_sem=send_sem.at[i], recv_sem=recv_sem.at[i],
+            device_id=to, device_id_type=MESH,
+        )
+        copy.start()
+        sent.append(copy)
+        return i
+
+    def arrive(i, dst):
+        pltpu.make_async_remote_copy(
+            src_ref=dst, dst_ref=dst, send_sem=send_sem.at[i], recv_sem=recv_sem.at[i],
+            device_id={"dp": d}, device_id_type=MESH,
+        ).wait_recv()
+
+    def col(k):
+        return ((z + k) % n_z) * COLS + x
+
+    to_x = {"dp": z * COLS + px}
+    to_y = {"mp": pm}
+    to_core = {"group": pg}
+    piece = voc // CHUNKS
+
+    def part(ref, c):
+        return ref.at[pl.ds(c * piece, piece), :]
+
+    s_z = {k: send(s_head, hs.at[d], {"dp": col(k)}) for k in range(1, n_z)}
+    s_x = {0: send(s_head, hs.at[d], to_x)}
+    rows_y = send(t_rows, rows_all.at[me], to_y)
+    t_z, t_x = {}, {}
+    for c in range(CHUNKS):
+        for k in range(1, n_z):
+            t_z[c, k] = send(part(t_head, c), part(ht.at[d], c), {"dp": col(k)})
+        t_x[c, 0] = send(part(t_head, c), part(ht.at[d], c), to_x)
+    rows_core = send(t_rows, rows_all.at[me], to_core)
+    gains = [send(t_gain, gain_all.at[me], peer) for peer in peers]
+
+    locals_[0].wait()
+    tile = 32
+
+    def student_tile(i, _):
+        at = pl.ds(pl.multiple_of(i * tile, tile), tile)
+        values = srow[at, :].astype(jnp.float32)
+        mean_square = jnp.mean(values * values, axis=-1, keepdims=True)
+        sn[at, :] = (values * lax.rsqrt(mean_square + epsilon) * s_gain[...]).astype(jnp.bfloat16)
+        return 0
+
+    lax.fori_loop(0, tok // tile, student_tile, 0)
+
+    for k in range(1, n_z):
+        slot = hs.at[col(n_z - k)]
+        arrive(s_z[k], slot)
+        s_x[k] = send(slot, slot, to_x)
+
+    def forward(c, k):
+        slot = part(ht.at[col(n_z - k)], c)
+        arrive(t_z[c, k], slot)
+        t_x[c, k] = send(slot, slot, to_x)
+
+    for k in range(1, n_z):
+        forward(0, k)
+    locals_[3].wait()
+    for k in range(n_z):
+        arrive(s_x[k], hs.at[((z + n_z - k) % n_z) * COLS + px])
+
+    def student_block(f, _):
+        at = pl.ds(pl.multiple_of(f * sf, sf), sf)
+        s_exp[...] += dot_nt(hs[f], sn[:, at])
+        return 0
+
+    s_exp[...] = jnp.zeros_like(s_exp)
+    lax.fori_loop(0, n_dp, student_block, 0)
+    for k in range(1, n_z):
+        forward(1, k)
+
+    def softmax_part(ref, row):
+        values = ref[...]
+        top = jnp.max(values, axis=0, keepdims=True)
+        exps = jnp.exp(values - top)
+        ref[...] = exps
+        stat[row : row + 1, :] = top
+        stat[row + 1 : row + 2, :] = jnp.sum(exps, axis=0, keepdims=True)
+
+    stat[...] = jnp.zeros_like(stat)
+    softmax_part(s_exp, 0)
+
+    arrive(rows_y, rows_all.at[peers_gm[0]])
+    rows_far = send(rows_all.at[peers_gm[0]], rows_all.at[peers_gm[0]], to_core)
+    for k in range(1, n_z):
+        forward(2, k)
+    locals_[1].wait()
+    locals_[4].wait()
+    for i in range(3):
+        arrive(gains[i], gain_all.at[peers_gm[i]])
+    arrive(rows_core, rows_all.at[peers_gm[1]])
+    arrive(rows_far, rows_all.at[peers_gm[2]])
+    width = t_rows.shape[1]
+
+    def teacher_tile(i, _):
+        at = pl.ds(pl.multiple_of(i * tile, tile), tile)
+        total = jnp.zeros((tile, 1), jnp.float32)
+        for j in range(blocks):
+            values = rows_all[j, at, :].astype(jnp.float32)
+            total += jnp.sum(values * values, axis=-1, keepdims=True)
+        scale = lax.rsqrt(total / (blocks * width) + epsilon)
+        for j in range(blocks):
+            values = rows_all[j, at, :].astype(jnp.float32)
+            tn[j, at, :] = (values * scale * gain_all[j, 0:1, :]).astype(jnp.bfloat16)
+        return 0
+
+    lax.fori_loop(0, tok // tile, teacher_tile, 0)
+
+    per = width // tf
+
+    def teacher_block(f):
+        at = pl.ds(pl.multiple_of((f % per) * tf, tf), tf)
+        t_exp[...] += dot_nt(ht[f], tn[f // per, :, at])
+
+    locals_[2].wait()
+    t_exp[...] = jnp.zeros_like(t_exp)
+
+    def own_column(i, _):
+        teacher_block(i * COLS + x)
+        return 0
+
+    lax.fori_loop(0, n_z, own_column, 0)
+    for k in range(n_z):
+        f = ((z + n_z - k) % n_z) * COLS + px
+        for c in range(CHUNKS):
+            arrive(t_x[c, k], part(ht.at[f], c))
+
+    def other_column(i, _):
+        teacher_block(i * COLS + px)
+        return 0
+
+    lax.fori_loop(0, n_z, other_column, 0)
+    softmax_part(t_exp, 2)
+
+    stats = [send(stat, stat_in.at[i], peers[i]) for i in range(3)]
+    for i in range(3):
+        arrive(stats[i], stat_in.at[i])
+
+    def factor(row):
+        tops = [stat[row : row + 1, :]] + [stat_in[i, row : row + 1, :] for i in range(3)]
+        sums = [stat[row + 1 : row + 2, :]] + [
+            stat_in[i, row + 1 : row + 2, :] for i in range(3)
+        ]
+        top = functools.reduce(jnp.maximum, tops)
+        total = sum(s * jnp.exp(t - top) for s, t in zip(sums, tops))
+        return live[0:1, :] * jnp.exp(tops[0] - top - jnp.log(total))
+
+    grad = s_exp[...] * factor(0) - t_exp[...] * factor(2)
+    lg_t[...] = grad.astype(jnp.bfloat16)
+    lg[...] = grad.T.astype(jnp.bfloat16)
+
+    def head_block(f):
+        at = pl.ds(pl.multiple_of(f * sf, sf), sf)
+        return jnp.dot(lg_t[...], sn[:, at], preferred_element_type=jnp.float32)
+
+    order = [*range(1, n_z), 0]
+    hx, hz = {}, {}
+    for k in order:
+        hx_out[k] = head_block(((z + k) % n_z) * COLS + px).astype(jnp.bfloat16)
+        hx[k] = send(hx_out.at[k], hx_in.at[k], to_x)
+
+    def row_block(t, dst, taken=None):
+        at = pl.ds(pl.multiple_of(t * own, own), own)
+
+        def step(f, _):
+            to = pl.ds(pl.multiple_of(f * sf, sf), sf)
+            value = jnp.dot(lg[at, :], hs[f], preferred_element_type=jnp.float32)
+            if taken is not None:
+                value += taken[:, to].astype(jnp.float32)
+            dst[:, to] = value.astype(dst.dtype)
+            return 0
+
+        lax.fori_loop(0, n_dp, step, 0)
+
+    rc = []
+    for i, mp in enumerate((pm, m)):
+        row_block(2 * pg + mp, rc_out.at[i])
+        rc.append(send(rc_out.at[i], rc_in.at[i], to_core))
+
+    for k in order[:-1]:
+        value = head_block(col(k))
+        arrive(hx[k], hx_in.at[k])
+        hz_out[k - 1] = (value + hx_in[k].astype(jnp.float32)).astype(jnp.bfloat16)
+        hz[k] = send(hz_out.at[k - 1], hz_in.at[k - 1], {"dp": col(k)})
+
+    arrive(rc[0], rc_in.at[0])
+    row_block(2 * g + pm, ry_out, rc_in.at[0])
+    ry = send(ry_out, ry_in, to_y)
+    value = head_block(d)
+    arrive(hx[0], hx_in.at[0])
+    h_acc[...] = value + hx_in[0].astype(jnp.float32)
+    arrive(rc[1], rc_in.at[1])
+    row_block(2 * g + m, r_acc, rc_in.at[1])
+    for k in range(1, n_z):
+        arrive(hz[k], hz_in.at[k - 1])
+    total = h_acc[...] + sum(hz_in[k].astype(jnp.float32) for k in range(n_z - 1))
+    h_acc[...] = total
+
+    def fold(values):
+        lanes = jnp.sum(values * values, axis=0, keepdims=True)
+        return sum(lanes[:, i : i + 128] for i in range(0, lanes.shape[1], 128))
+
+    sq[...] = jnp.zeros_like(sq)
+    sq[0:1, :] = fold(total)
+    arrive(ry, ry_in)
+
+    def row_sum(i, acc):
+        at = pl.ds(pl.multiple_of(i * tile, tile), tile)
+        values = r_acc[at, :] + ry_in[at, :].astype(jnp.float32)
+        r_acc[at, :] = values
+        return acc + fold(values)
+
+    sq[1:2, :] = lax.fori_loop(0, own // tile, row_sum, jnp.zeros((1, 128), jnp.float32))
+
+    first = [send(sq, sq_in.at[i], peers[i]) for i in range(3)]
+    for i in range(3):
+        arrive(first[i], sq_in.at[i])
+    sq2[...] = sq[...] + sq_in[0] + sq_in[1] + sq_in[2]
+    second = [send(sq2, sq2_in.at[k - 1], {"dp": (d + k) % n_dp}) for k in range(1, n_dp)]
+    for k in range(1, n_dp):
+        arrive(second[k - 1], sq2_in.at[k - 1])
+    squares = jnp.sum(sq2[...] + jnp.sum(sq2_in[...], axis=0), axis=1, keepdims=True)
+    devices = n_dp * blocks
+    head_out[...] = (
+        h_acc[...] * lax.rsqrt(squares[0:1, :] / (voc * sf * devices) + epsilon)
+    ).astype(jnp.bfloat16)
+    row_out[...] = (
+        r_acc[...] * lax.rsqrt(squares[1:2, :] / (own * ds * devices) + epsilon)
+    ).astype(jnp.bfloat16)
+    for copy in sent:
+        copy.wait_send()
+
+
+def fused(
+    teacher_rows, teacher_gain, teacher_head, student_rows, student_gain, student_head, lengths
+):
+    n_dp = lax.axis_size("dp")
+    tok, width = teacher_rows.shape
+    voc, tf = teacher_head.shape
+    ds, sf = student_rows.shape[1], student_head.shape[1]
+    n_z, own = n_dp // COLS, tok // 4
+    position = jnp.arange(tok, dtype=jnp.int32) % LMAX
+    live = (position < jnp.repeat(lengths, LMAX, total_repeat_length=tok)).astype(jnp.float32)
+    bf, f32 = jnp.bfloat16, jnp.float32
+    copies = 3 + 2 * n_z - 1 + CHUNKS * (2 * n_z - 1) + 3 + 3 + 2 * n_z - 1 + 3 + 3 + n_dp - 1
+    anywhere, vmem = pl.BlockSpec(memory_space=pl.ANY), pl.BlockSpec(memory_space=pltpu.VMEM)
+    return pl.pallas_call(
+        functools.partial(step_kernel, n_dp),
+        out_shape=(
+            jax.ShapeDtypeStruct((voc, sf), bf),
+            jax.ShapeDtypeStruct((own, ds), bf),
+        ),
+        in_specs=[anywhere, anywhere, anywhere, anywhere, vmem, anywhere, vmem],
+        out_specs=(vmem, vmem),
+        scratch_shapes=[
+            pltpu.VMEM((4, tok, width), bf),
+            pltpu.VMEM((4, 8, width), f32),
+            pltpu.VMEM((n_dp, voc, tf), bf),
+            pltpu.VMEM((n_dp, voc, sf), bf),
+            pltpu.VMEM((tok, ds), bf),
+            pltpu.VMEM((tok, ds), bf),
+            pltpu.VMEM((4, tok, width), bf),
+            pltpu.VMEM((voc, tok), f32),
+            pltpu.VMEM((voc, tok), f32),
+            pltpu.VMEM((voc, tok), bf),
+            pltpu.VMEM((tok, voc), bf),
+            pltpu.VMEM((8, tok), f32),
+            pltpu.VMEM((3, 8, tok), f32),
+            pltpu.VMEM((n_z, voc, sf), bf),
+            pltpu.VMEM((n_z, voc, sf), bf),
+            pltpu.VMEM((n_z - 1, voc, sf), bf),
+            pltpu.VMEM((n_z - 1, voc, sf), bf),
+            pltpu.VMEM((voc, sf), f32),
+            pltpu.VMEM((2, own, ds), bf),
+            pltpu.VMEM((2, own, ds), bf),
+            pltpu.VMEM((own, ds), bf),
+            pltpu.VMEM((own, ds), bf),
+            pltpu.VMEM((own, ds), f32),
+            pltpu.VMEM((8, 128), f32),
+            pltpu.VMEM((3, 8, 128), f32),
+            pltpu.VMEM((8, 128), f32),
+            pltpu.VMEM((n_dp - 1, 8, 128), f32),
+            pltpu.SemaphoreType.DMA((copies,)),
+            pltpu.SemaphoreType.DMA((copies,)),
+            pltpu.SemaphoreType.DMA((5,)),
+        ],
+        compiler_params=pltpu.CompilerParams(
+            collective_id=0, has_side_effects=True, vmem_limit_bytes=56 << 20
+        ),
+    )(
+        teacher_rows,
+        jnp.broadcast_to(teacher_gain.astype(f32), (8, width)),
+        teacher_head,
+        student_rows,
+        student_gain.astype(f32)[None, :],
+        student_head,
+        jnp.broadcast_to(live, (8, tok)),
+    )
+
+
+def step(*args):
+    t_rows, _, t_head, s_rows, _, s_head, _ = args
+    fits = (
+        (lax.axis_size("group"), lax.axis_size("mp"), lax.axis_size("dp") % COLS) == (2, 2, 0)
+        and lax.axis_size("dp") <= 16
+        and t_head.shape[1] % 128 == 0
+        and s_head.shape[1] % 128 == 0
+        and t_rows.shape[1] % t_head.shape[1] == 0
+        and t_head.shape[0] % (16 * CHUNKS) == 0
+        and s_rows.shape[0] % 128 == 0
+    )
+    return fused(*args) if fits else body(*args)
+
+
 def solution(mesh):
     placed = (
         P("dp", ("group", "mp")),
@@ -107,7 +487,7 @@
         P("dp"),
     )
     return jax.shard_map(
-        body,
+        step,
         mesh=mesh,
         in_specs=placed,
         out_specs=(P(("group", "mp"), "dp"), P(("dp", "group", "mp"), None)),

time: 359 us -> 136 us (0.38)
  waiting for transfers between devices: 246 us -> 0 us
  Pallas kernels: 0 us -> 127 us
  blocking collectives: 63.4 us -> 0 us
  matrix products: 18.8 us -> 0 us
  between operations: 15.9 us -> 1.29 us
  other arithmetic: 13.7 us -> 1.29 us
  local copies, waits for them, and re-layouts: 0.84 us -> 5.51 us
    all_gather x3 -> x0, waiting for transfers between devices: 148 us -> none  [the longest x1 66.5 us: body(): lax.all_gather(teacher_head, 'dp', axis=1, tiled=True)]
    pallas_call x0 -> x1, Pallas kernels: none -> 127 us  [fused(): pl.pallas_call(functools.partial(step_kernel, n_dp), out_shape=(jax.Shape...]
    reduce_scatter x2 -> x0, waiting for transfers between devices: 96.5 us -> none  [the longest x1 61.9 us: body(): lax.psum_scatter(lax.dot_general(student_normed, logit_grad, (((0,), (0,)...]
    psum x3 -> x0, blocking collectives: 56.9 us -> none  [the longest x1 39.6 us: body(): lax.psum((jnp.sum(head_grad * head_grad), jnp.sum(row_grad * row_grad)),...]
    dot_general x4 -> x0, matrix products: 18.8 us -> none  [the longest x2 10.9 us: against(): lax.dot_general(rows, weights, (((1,), (1,)), ((), ())), preferred_elemen...]
    reduce_sum x5 -> x0, other arithmetic: 8.08 us -> none  [the longest x1 2.32 us: normalize(): mean_square = jnp.mean(values * values, axis=-1, keepdims=True)]
    pmax x1 -> x0, blocking collectives: 6.44 us -> none  [body(): lax.pmax((jnp.max(teacher_logits, axis=1), jnp.max(student_logits, axis=1...]
    convert_element_type x7 -> x1, other arithmetic: 5.61 us -> 0.01 us  [fused(): (position < jnp.repeat(lengths, LMAX, total_repeat_length=tok)).astype(jn...]
  transfers between devices with their start and end apart: 5 -> 0, of which waited for: 5 -> 0; matrix products, arithmetic and copies ran while one was open for 4% -> 0% of each run, Pallas kernels for 0% -> 0%
where the time goes in v1:
time: 136 us; the launch traced here: 135 us
  Pallas kernels  127 us (93%)
  local copies, waits for them, and re-layouts  5.51 us (4%)
    pallas_call x1, Pallas kernels, fused(): pl.pallas_call(functools.partial(step_kernel, n_dp), out_shape=(jax.Shape...  127 us
    unnamed x2, local copies, waits for them, and re-layouts  3.6 us

profile of v1, /device:TPU:0, one launch (start us, length us, event | category | flops | bytes accessed | tf_op | source)
XLA Modules:
  0.0 135.3 jit_solution(5319544834956789950)
XLA Ops:
  1.3 1.3 broadcast_in_dim.21
  2.6 0.6 broadcast_in_dim.20.live
  3.2 1.3 broadcast_in_dim.17.t_gain
  4.5 127.2 %shard_map.89 = (bf16[384,256]{1,0:T(8,128)(2,1)}, bf16[160,2048]{1,0:T(8,128)(2,1)}) custom-call(bf16[640,1280]{1,0:T(8,128)(2,1)} %t_rows.1, f32[8,1280]{1,0:T(8,128)} %broadcast_in_dim.17.t_gain, bf16[384,640]{1,0:T(8,128)(2,1)} %t_head.1, bf16[640,2048]{1,0:T(8,128)(2,1)} %s_rows.1, f32[1,2048]{1,0:T(1,128)} %bitcast.3, bf16[384,256]{1,0:T(8,128)(2,1)} %s_head.1, ...), custom_call_target="tpu_custom_call" | custom-call | tf_op jit(solution)/shard_map/pallas_call | solution.py:411
  131.7 1.6 %copy.12 = bf16[384,256]{1,0:T(8,128)(2,1)} copy(bf16[384,256]{1,0:T(8,128)(2,1)} %get-tuple-element.28) | data formatting | bytes 393216
  133.3 2.0 %copy.13 = bf16[160,2048]{1,0:T(8,128)(2,1)} copy(bf16[160,2048]{1,0:T(8,128)(2,1)} %get-tuple-element.29) | data formatting | bytes 1310720
  (1 shorter events, 0.0 us)

commit v2 on v1

--- a/solution.py
+++ b/solution.py
@@ -111,7 +111,7 @@
 
 def step_kernel(
     n_dp,
-    t_rows, t_gain, t_head, s_rows, s_gain, s_head, live,
+    t_rows, t_gain, t_head, s_rows, s_gain, s_head, lengths,
     head_out, row_out,
     rows_all, gain_all, ht, hs, srow, sn, tn, t_exp, s_exp, lg_t, lg,
     stat, stat_in, hx_out, hx_in, hz_out, hz_in, h_acc,
@@ -147,24 +147,29 @@
                 (t_rows, rows_all.at[me]),
                 (t_head, ht.at[d]),
                 (s_head, hs.at[d]),
-                (t_gain, gain_all.at[me]),
             ]
         )
     ]
     for copy in locals_:
         copy.start()
+    gain_all[me] = jnp.broadcast_to(
+        t_gain[...].astype(jnp.float32).reshape(1, -1), gain_all.shape[1:]
+    )
     pl.semaphore_wait(barrier, 3 + n_dp - 1)
 
-    sent = []
-
-    def send(src, dst, to):
+    sent, always = [], None
+
+    def send(src, dst, to, when=always):
         i = len(sent)
         copy = pltpu.make_async_remote_copy(
             src_ref=src, dst_ref=dst, send_sem=send_sem.at[i], recv_sem=recv_sem.at[i],
             device_id=to, device_id_type=MESH,
         )
-        copy.start()
-        sent.append(copy)
+        if when is None:
+            copy.start()
+        else:
+            pl.when(when)(copy.start)
+        sent.append((copy, when))
         return i
 
     def arrive(i, dst):
@@ -184,44 +189,79 @@
     def part(ref, c):
         return ref.at[pl.ds(c * piece, piece), :]
 
-    s_z = {k: send(s_head, hs.at[d], {"dp": col(k)}) for k in range(1, n_z)}
-    s_x = {0: send(s_head, hs.at[d], to_x)}
-    rows_y = send(t_rows, rows_all.at[me], to_y)
-    t_z, t_x = {}, {}
-    for c in range(CHUNKS):
-        for k in range(1, n_z):
-            t_z[c, k] = send(part(t_head, c), part(ht.at[d], c), {"dp": col(k)})
-        t_x[c, 0] = send(part(t_head, c), part(ht.at[d], c), to_x)
+    parts = [(s_head, hs, None)] + [(t_head, ht, c) for c in range(CHUNKS)]
+    ways = (1, -1)
+
+    def view(ref, c):
+        return ref if c is None else part(ref, c)
+
+    def inside(at):
+        return (at >= 0) & (at < n_z)
+
+    along, across = {}, {}
+    for p, (src, dst, c) in enumerate(parts):
+        for way in ways:
+            along[way, 0, p] = send(
+                view(src, c), view(dst.at[d], c), {"dp": (z + way) % n_z * COLS + x},
+                inside(z + way),
+            )
+        across[p] = send(view(src, c), view(dst.at[d], c), to_x)
+        if p == 0:
+            rows_y = send(t_rows, rows_all.at[me], to_y)
     rows_core = send(t_rows, rows_all.at[me], to_core)
-    gains = [send(t_gain, gain_all.at[me], peer) for peer in peers]
+    gains = [send(gain_all.at[me], gain_all.at[me], peer) for peer in peers]
+
+    def origin(way, hop):
+        return z - way * (hop + 1)
+
+    def block(way, hop, column):
+        return (origin(way, hop) + n_z) % n_z * COLS + column
+
+    def forward(hop, p):
+        _, dst, c = parts[p]
+        for way in ways:
+            here = inside(origin(way, hop))
+            slot = view(dst.at[block(way, hop, x)], c)
+
+            @pl.when(here)
+            def _():
+                arrive(along[way, hop, p], slot)
+
+            if hop < n_z - 2:
+                along[way, hop + 1, p] = send(
+                    slot, slot, {"dp": (z + way + n_z) % n_z * COLS + x}, here & inside(z + way)
+                )
+            across[way, hop, p] = send(slot, slot, to_x, here)
 
     locals_[0].wait()
     tile = 32
+
+    gain = s_gain[...].astype(jnp.float32).reshape(1, -1)
 
     def student_tile(i, _):
         at = pl.ds(pl.multiple_of(i * tile, tile), tile)
         values = srow[at, :].astype(jnp.float32)
         mean_square = jnp.mean(values * values, axis=-1, keepdims=True)
-        sn[at, :] = (values * lax.rsqrt(mean_square + epsilon) * s_gain[...]).astype(jnp.bfloat16)
+        sn[at, :] = (values * lax.rsqrt(mean_square + epsilon) * gain).astype(jnp.bfloat16)
         return 0
 
     lax.fori_loop(0, tok // tile, student_tile, 0)
 
-    for k in range(1, n_z):
-        slot = hs.at[col(n_z - k)]
-        arrive(s_z[k], slot)
-        s_x[k] = send(slot, slot, to_x)
-
-    def forward(c, k):
-        slot = part(ht.at[col(n_z - k)], c)
-        arrive(t_z[c, k], slot)
-        t_x[c, k] = send(slot, slot, to_x)
-
-    for k in range(1, n_z):
-        forward(0, k)
+    for hop in range(n_z - 1):
+        for p in range(len(parts)):
+            forward(hop, p)
+        if hop == n_z - 3:
+            arrive(rows_y, rows_all.at[peers_gm[0]])
+            rows_far = send(rows_all.at[peers_gm[0]], rows_all.at[peers_gm[0]], to_core)
+
     locals_[3].wait()
-    for k in range(n_z):
-        arrive(s_x[k], hs.at[((z + n_z - k) % n_z) * COLS + px])
+    arrive(across[0], hs.at[z * COLS + px])
+    for hop in range(n_z - 1):
+        for way in ways:
+
+            @pl.when(inside(origin(way, hop)))
+            def _():
+                arrive(across[way, hop, 0], hs.at[block(way, hop, px)])
 
     def student_block(f, _):
         at = pl.ds(pl.multiple_of(f * sf, sf), sf)
@@ -230,8 +270,6 @@
 
     s_exp[...] = jnp.zeros_like(s_exp)
     lax.fori_loop(0, n_dp, student_block, 0)
-    for k in range(1, n_z):
-        forward(1, k)
 
     def softmax_part(ref, row):
         values = ref[...]
@@ -244,12 +282,7 @@
     stat[...] = jnp.zeros_like(stat)
     softmax_part(s_exp, 0)
 
-    arrive(rows_y, rows_all.at[peers_gm[0]])
-    rows_far = send(rows_all.at[peers_gm[0]], rows_all.at[peers_gm[0]], to_core)
-    for k in range(1, n_z):
-        forward(2, k)
     locals_[1].wait()
-    locals_[4].wait()
     for i in range(3):
         arrive(gains[i], gain_all.at[peers_gm[i]])
     arrive(rows_core, rows_all.at[peers_gm[1]])
@@ -284,21 +317,27 @@
         return 0
 
     lax.fori_loop(0, n_z, own_column, 0)
-    for k in range(n_z):
-        f = ((z + n_z - k) % n_z) * COLS + px
-        for c in range(CHUNKS):
-            arrive(t_x[c, k], part(ht.at[f], c))
-
-    def other_column(i, _):
-        teacher_block(i * COLS + px)
-        return 0
-
-    lax.fori_loop(0, n_z, other_column, 0)
+    for p in range(1, len(parts)):
+        arrive(across[p], part(ht.at[z * COLS + px], parts[p][2]))
+    teacher_block(z * COLS + px)
+    for hop in range(n_z - 1):
+        for way in ways:
+
+            @pl.when(inside(origin(way, hop)))
+            def _():
+                f = block(way, hop, px)
+                for p in range(1, len(parts)):
+                    arrive(across[way, hop, p], part(ht.at[f], parts[p][2]))
+                teacher_block(f)
+
     softmax_part(t_exp, 2)
 
     stats = [send(stat, stat_in.at[i], peers[i]) for i in range(3)]
     for i in range(3):
         arrive(stats[i], stat_in.at[i])
+
+    position = lax.broadcasted_iota(jnp.int32, (1, tok), 1) % LMAX
+    live = (position < lengths[0]).astype(jnp.float32)
 
     def factor(row):
         tops = [stat[row : row + 1, :]] + [stat_in[i, row : row + 1, :] for i in range(3)]
@@ -307,7 +346,7 @@
         ]
         top = functools.reduce(jnp.maximum, tops)
         total = sum(s * jnp.exp(t - top) for s, t in zip(sums, tops))
-        return live[0:1, :] * jnp.exp(tops[0] - top - jnp.log(total))
+        return live * jnp.exp(tops[0] - top - jnp.log(total))
 
     grad = s_exp[...] * factor(0) - t_exp[...] * factor(2)
     lg_t[...] = grad.astype(jnp.bfloat16)
@@ -316,12 +355,6 @@
     def head_block(f):
         at = pl.ds(pl.multiple_of(f * sf, sf), sf)
         return jnp.dot(lg_t[...], sn[:, at], preferred_element_type=jnp.float32)
-
-    order = [*range(1, n_z), 0]
-    hx, hz = {}, {}
-    for k in order:
-        hx_out[k] = head_block(((z + k) % n_z) * COLS + px).astype(jnp.bfloat16)
-        hx[k] = send(hx_out.at[k], hx_in.at[k], to_x)
 
     def row_block(t, dst, taken=None):
         at = pl.ds(pl.multiple_of(t * own, own), own)
@@ -336,20 +369,25 @@
 
         lax.fori_loop(0, n_dp, step, 0)
 
-    rc = []
-    for i, mp in enumerate((pm, m)):
+    def to_mate(i, mp):
         row_block(2 * pg + mp, rc_out.at[i])
-        rc.append(send(rc_out.at[i], rc_in.at[i], to_core))
-
+        return send(rc_out.at[i], rc_in.at[i], to_core)
+
+    order = [*range(1, n_z), 0]
+    hx, hz = {}, {}
+    rc = [to_mate(0, pm)]
+    for k in order:
+        hx_out[k] = head_block(((z + k) % n_z) * COLS + px).astype(jnp.bfloat16)
+        hx[k] = send(hx_out.at[k], hx_in.at[k], to_x)
+    rc.append(to_mate(1, m))
+    arrive(rc[0], rc_in.at[0])
+    row_block(2 * g + pm, ry_out, rc_in.at[0])
+    ry = send(ry_out, ry_in, to_y)
     for k in order[:-1]:
         value = head_block(col(k))
         arrive(hx[k], hx_in.at[k])
         hz_out[k - 1] = (value + hx_in[k].astype(jnp.float32)).astype(jnp.bfloat16)
         hz[k] = send(hz_out.at[k - 1], hz_in.at[k - 1], {"dp": col(k)})
-
-    arrive(rc[0], rc_in.at[0])
-    row_block(2 * g + pm, ry_out, rc_in.at[0])
-    ry = send(ry_out, ry_in, to_y)
     value = head_block(d)
     arrive(hx[0], hx_in.at[0])
     h_acc[...] = value + hx_in[0].astype(jnp.float32)
@@ -391,8 +429,11 @@
     row_out[...] = (
         r_acc[...] * lax.rsqrt(squares[1:2, :] / (own * ds * devices) + epsilon)
     ).astype(jnp.bfloat16)
-    for copy in sent:
-        copy.wait_send()
+    for copy, when in sent:
+        if when is None:
+            copy.wait_send()
+        else:
+            pl.when(when)(copy.wait_send)
 
 
 def fused(
@@ -403,18 +444,18 @@
     voc, tf = teacher_head.shape
     ds, sf = student_rows.shape[1], student_head.shape[1]
     n_z, own = n_dp // COLS, tok // 4
-    position = jnp.arange(tok, dtype=jnp.int32) % LMAX
-    live = (position < jnp.repeat(lengths, LMAX, total_repeat_length=tok)).astype(jnp.float32)
     bf, f32 = jnp.bfloat16, jnp.float32
-    copies = 3 + 2 * n_z - 1 + CHUNKS * (2 * n_z - 1) + 3 + 3 + 2 * n_z - 1 + 3 + 3 + n_dp - 1
+    hops = (1 + CHUNKS) * (n_z - 1) * 4 + (1 + CHUNKS)
+    copies = 3 + hops + 3 + 3 + 2 * n_z - 1 + 3 + 3 + n_dp - 1
     anywhere, vmem = pl.BlockSpec(memory_space=pl.ANY), pl.BlockSpec(memory_space=pltpu.VMEM)
+    scalars = pl.BlockSpec(memory_space=pltpu.SMEM)
     return pl.pallas_call(
         functools.partial(step_kernel, n_dp),
         out_shape=(
             jax.ShapeDtypeStruct((voc, sf), bf),
             jax.ShapeDtypeStruct((own, ds), bf),
         ),
-        in_specs=[anywhere, anywhere, anywhere, anywhere, vmem, anywhere, vmem],
+        in_specs=[anywhere, vmem, anywhere, anywhere, vmem, anywhere, scalars],
         out_specs=(vmem, vmem),
         scratch_shapes=[
             pltpu.VMEM((4, tok, width), bf),
@@ -446,24 +487,24 @@
             pltpu.VMEM((n_dp - 1, 8, 128), f32),
             pltpu.SemaphoreType.DMA((copies,)),
             pltpu.SemaphoreType.DMA((copies,)),
-            pltpu.SemaphoreType.DMA((5,)),
+            pltpu.SemaphoreType.DMA((4,)),
         ],
         compiler_params=pltpu.CompilerParams(
             collective_id=0, has_side_effects=True, vmem_limit_bytes=56 << 20
         ),
     )(
         teacher_rows,
-        jnp.broadcast_to(teacher_gain.astype(f32), (8, width)),
+        teacher_gain,
         teacher_head,
         student_rows,
-        student_gain.astype(f32)[None, :],
+        student_gain,
         student_head,
-        jnp.broadcast_to(live, (8, tok)),
+        lengths,
     )
 
 
 def step(*args):
-    t_rows, _, t_head, s_rows, _, s_head, _ = args
+    t_rows, _, t_head, s_rows, _, s_head, lengths = args
     fits = (
         (lax.axis_size("group"), lax.axis_size("mp"), lax.axis_size("dp") % COLS) == (2, 2, 0)
         and lax.axis_size("dp") <= 16
@@ -472,6 +513,7 @@
         and t_rows.shape[1] % t_head.shape[1] == 0
         and t_head.shape[0] % (16 * CHUNKS) == 0
         and s_rows.shape[0] % 128 == 0
+        and lengths.shape[0] == 1
     )
     return fused(*args) if fits else body(*args)
 

time: 136 us -> 115 us (0.85)
  Pallas kernels: 127 us -> 110 us
  local copies, waits for them, and re-layouts: 5.51 us -> 3.6 us
    pallas_call x1, Pallas kernels: 127 us -> 110 us  [fused(): pl.pallas_call(functools.partial(step_kernel, n_dp), out_shape=(jax.Shape...]
    broadcast_in_dim x2 -> x0, local copies, waits for them, and re-layouts: 1.91 us -> none  [the longest x1 1.31 us: fused(): jnp.broadcast_to(teacher_gain.astype(f32), (8, width))]
where the time goes in v2:
time: 115 us
  Pallas kernels  110 us (96%)
  local copies, waits for them, and re-layouts  3.6 us (3%)
  between operations  1.29 us (1%)
    pallas_call x1, Pallas kernels, fused(): pl.pallas_call(functools.partial(step_kernel, n_dp), out_shape=(jax.Shape...  110 us
    unnamed x2, local copies, waits for them, and re-layouts  3.6 us

profile of v2, /device:TPU:0, one launch (start us, length us, event | category | flops | bytes accessed | tf_op | source)
XLA Modules:
  0.0 114.6 jit_solution(13808752925215725255)
XLA Ops:
  1.3 109.7 %shard_map.86 = (bf16[384,256]{1,0:T(8,128)(2,1)}, bf16[160,2048]{1,0:T(8,128)(2,1)}) custom-call(bf16[640,1280]{1,0:T(8,128)(2,1)} %t_rows.1, bf16[1280]{0:T(1024)(128)(2,1)} %t_gain.1, bf16[384,640]{1,0:T(8,128)(2,1)} %t_head.1, bf16[640,2048]{1,0:T(8,128)(2,1)} %s_rows.1, bf16[2048]{0:T(1024)(128)(2,1)} %s_gain.1, bf16[384,256]{1,0:T(8,128)(2,1)} %s_head.1, ...), custom_call_target="tpu_custom_call" | custom-call | tf_op jit(solution)/shard_map/pallas_call | solution.py:452
  111.0 1.6 %copy.12 = bf16[384,256]{1,0:T(8,128)(2,1)} copy(bf16[384,256]{1,0:T(8,128)(2,1)} %get-tuple-element.4) | data formatting | bytes 393216
  112.6 2.0 %copy.13 = bf16[160,2048]{1,0:T(8,128)(2,1)} copy(bf16[160,2048]{1,0:T(8,128)(2,1)} %get-tuple-element.5) | data formatting | bytes 1310720

commit v3 on v2

--- a/solution.py
+++ b/solution.py
@@ -231,7 +231,57 @@
                 along[way, hop + 1, p] = send(
                     slot, slot, {"dp": (z + way + n_z) % n_z * COLS + x}, here & inside(z + way)
                 )
-            across[way, hop, p] = send(slot, slot, to_x, here)
+            if hop == 0:
+                across[way, hop, p] = send(slot, slot, to_x, here & ~from_end(way))
+            elif hop < n_z - 2 or p not in bent:
+                across[way, hop, p] = send(slot, slot, to_x, here)
+
+    bent = (2, 3)
+    turned, bend = {}, {}
+
+    def from_end(way):
+        return ~inside(origin(way, 0) - way)
+
+    def arrive_if(when, i, dst):
+        @pl.when(when)
+        def _():
+            arrive(i, dst)
+
+    def turn(p):
+        _, dst, c = parts[p]
+        slot = view(dst.at[z * COLS + px], c)
+        arrive(across[p], slot)
+        for way in ways:
+            turned[way, p] = send(
+                slot, slot, {"dp": (z + way + n_z) % n_z * COLS + x},
+                inside(z + way) & ~inside(z - way),
+            )
+
+    def through(hop, way):
+        return inside(origin(way, hop)) & inside(z + way)
+
+    def bend_on(p):
+        _, dst, c = parts[p]
+        for way in ways:
+            slot = view(dst.at[block(way, n_z - 3, px)], c)
+            arrive_if(through(n_z - 3, way), across[way, n_z - 3, p], slot)
+            bend[way, p] = send(
+                slot, slot, {"dp": (z + way + n_z) % n_z * COLS + x}, through(n_z - 3, way)
+            )
+
+    def arrive_across(way, hop, p):
+        _, dst, c = parts[p]
+        slot = view(dst.at[block(way, hop, px)], c)
+        here = inside(origin(way, hop))
+        if hop == 0:
+            arrive_if(here & from_end(way), turned[way, p], slot)
+            arrive_if(here & ~from_end(way), across[way, hop, p], slot)
+        elif p not in bent or hop < n_z - 3:
+            arrive_if(here, across[way, hop, p], slot)
+        elif hop == n_z - 3:
+            arrive_if(here & ~inside(z + way), across[way, hop, p], slot)
+        else:
+            arrive_if(here, bend[way, p], slot)
 
     locals_[0].wait()
     tile = 32
@@ -248,20 +298,21 @@
     lax.fori_loop(0, tok // tile, student_tile, 0)
 
     for hop in range(n_z - 1):
+        if hop == n_z - 2:
+            for p in bent:
+                bend_on(p)
         for p in range(len(parts)):
             forward(hop, p)
+            if hop == 0:
+                turn(p)
         if hop == n_z - 3:
             arrive(rows_y, rows_all.at[peers_gm[0]])
             rows_far = send(rows_all.at[peers_gm[0]], rows_all.at[peers_gm[0]], to_core)
 
     locals_[3].wait()
-    arrive(across[0], hs.at[z * COLS + px])
     for hop in range(n_z - 1):
         for way in ways:
-
-            @pl.when(inside(origin(way, hop)))
-            def _():
-                arrive(across[way, hop, 0], hs.at[block(way, hop, px)])
+            arrive_across(way, hop, 0)
 
     def student_block(f, _):
         at = pl.ds(pl.multiple_of(f * sf, sf), sf)
@@ -317,18 +368,15 @@
         return 0
 
     lax.fori_loop(0, n_z, own_column, 0)
-    for p in range(1, len(parts)):
-        arrive(across[p], part(ht.at[z * COLS + px], parts[p][2]))
     teacher_block(z * COLS + px)
     for hop in range(n_z - 1):
         for way in ways:
+            for p in range(1, len(parts)):
+                arrive_across(way, hop, p)
 
             @pl.when(inside(origin(way, hop)))
             def _():
-                f = block(way, hop, px)
-                for p in range(1, len(parts)):
-                    arrive(across[way, hop, p], part(ht.at[f], parts[p][2]))
-                teacher_block(f)
+                teacher_block(block(way, hop, px))
 
     softmax_part(t_exp, 2)
 
@@ -445,7 +493,7 @@
     ds, sf = student_rows.shape[1], student_head.shape[1]
     n_z, own = n_dp // COLS, tok // 4
     bf, f32 = jnp.bfloat16, jnp.float32
-    hops = (1 + CHUNKS) * (n_z - 1) * 4 + (1 + CHUNKS)
+    hops = (1 + CHUNKS) * ((n_z - 1) * 4 + 3)
     copies = 3 + hops + 3 + 3 + 2 * n_z - 1 + 3 + 3 + n_dp - 1
     anywhere, vmem = pl.BlockSpec(memory_space=pl.ANY), pl.BlockSpec(memory_space=pltpu.VMEM)
     scalars = pl.BlockSpec(memory_space=pltpu.SMEM)
@@ -507,7 +555,7 @@
     t_rows, _, t_head, s_rows, _, s_head, lengths = args
     fits = (
         (lax.axis_size("group"), lax.axis_size("mp"), lax.axis_size("dp") % COLS) == (2, 2, 0)
-        and lax.axis_size("dp") <= 16
+        and 4 * COLS <= lax.axis_size("dp") <= 16
         and t_head.shape[1] % 128 == 0
         and s_head.shape[1] % 128 == 0
         and t_rows.shape[1] % t_head.shape[1] == 0

time: 115 us -> 113 us (0.983)
  Pallas kernels: 110 us -> 108 us
    pallas_call x1, Pallas kernels: 110 us -> 108 us  [fused(): pl.pallas_call(functools.partial(step_kernel, n_dp), out_shape=(jax.Shape...]
where the time goes in v3:
time: 113 us; the launch traced here: 112 us
  Pallas kernels  108 us (96%)
  local copies, waits for them, and re-layouts  3.6 us (3%)
  between operations  1.29 us (1%)
    pallas_call x1, Pallas kernels, fused(): pl.pallas_call(functools.partial(step_kernel, n_dp), out_shape=(jax.Shape...  108 us
    unnamed x2, local copies, waits for them, and re-layouts  3.6 us

profile of v3, /device:TPU:0, one launch (start us, length us, event | category | flops | bytes accessed | tf_op | source)
XLA Modules:
  0.0 112.4 jit_solution(18123232835398980223)
XLA Ops:
  1.3 107.5 %shard_map.86 = (bf16[384,256]{1,0:T(8,128)(2,1)}, bf16[160,2048]{1,0:T(8,128)(2,1)}) custom-call(bf16[640,1280]{1,0:T(8,128)(2,1)} %t_rows.1, bf16[1280]{0:T(1024)(128)(2,1)} %t_gain.1, bf16[384,640]{1,0:T(8,128)(2,1)} %t_head.1, bf16[640,2048]{1,0:T(8,128)(2,1)} %s_rows.1, bf16[2048]{0:T(1024)(128)(2,1)} %s_gain.1, bf16[384,256]{1,0:T(8,128)(2,1)} %s_head.1, ...), custom_call_target="tpu_custom_call" | custom-call | tf_op jit(solution)/shard_map/pallas_call | solution.py:500
  108.8 1.6 %copy.12 = bf16[384,256]{1,0:T(8,128)(2,1)} copy(bf16[384,256]{1,0:T(8,128)(2,1)} %get-tuple-element.4) | data formatting | bytes 393216
  110.4 2.0 %copy.13 = bf16[160,2048]{1,0:T(8,128)(2,1)} copy(bf16[160,2048]{1,0:T(8,128)(2,1)} %get-tuple-element.5) | data formatting | bytes 1310720

commit v4 on v3

--- a/solution.py
+++ b/solution.py
@@ -297,30 +297,20 @@
 
     lax.fori_loop(0, tok // tile, student_tile, 0)
 
-    for hop in range(n_z - 1):
-        if hop == n_z - 2:
-            for p in bent:
-                bend_on(p)
-        for p in range(len(parts)):
-            forward(hop, p)
-            if hop == 0:
-                turn(p)
-        if hop == n_z - 3:
-            arrive(rows_y, rows_all.at[peers_gm[0]])
-            rows_far = send(rows_all.at[peers_gm[0]], rows_all.at[peers_gm[0]], to_core)
-
-    locals_[3].wait()
-    for hop in range(n_z - 1):
-        for way in ways:
-            arrive_across(way, hop, 0)
-
-    def student_block(f, _):
+    def student_block(f):
         at = pl.ds(pl.multiple_of(f * sf, sf), sf)
         s_exp[...] += dot_nt(hs[f], sn[:, at])
-        return 0
-
-    s_exp[...] = jnp.zeros_like(s_exp)
-    lax.fori_loop(0, n_dp, student_block, 0)
+
+    def student_blocks(which):
+        def step(i, _):
+            @pl.when(which(i))
+            def _():
+                student_block(i * COLS + x)
+                student_block(i * COLS + px)
+
+            return 0
+
+        lax.fori_loop(0, n_z, step, 0)
 
     def softmax_part(ref, row):
         values = ref[...]
@@ -330,9 +320,21 @@
         stat[row : row + 1, :] = top
         stat[row + 1 : row + 2, :] = jnp.sum(exps, axis=0, keepdims=True)
 
-    stat[...] = jnp.zeros_like(stat)
-    softmax_part(s_exp, 0)
-
+    for hop in range(n_z - 2):
+        for p in range(len(parts)):
+            forward(hop, p)
+            if hop == 0:
+                turn(p)
+    arrive(rows_y, rows_all.at[peers_gm[0]])
+    rows_far = send(rows_all.at[peers_gm[0]], rows_all.at[peers_gm[0]], to_core)
+
+    near = n_z - 2
+    locals_[3].wait()
+    for hop in range(near):
+        for way in ways:
+            arrive_across(way, hop, 0)
+    s_exp[...] = jnp.zeros_like(s_exp)
+    student_blocks(lambda i: (i - z <= near) & (z - i <= near))
     locals_[1].wait()
     for i in range(3):
         arrive(gains[i], gain_all.at[peers_gm[i]])
@@ -354,6 +356,16 @@
 
     lax.fori_loop(0, tok // tile, teacher_tile, 0)
 
+    for p in bent:
+        bend_on(p)
+    for p in range(len(parts)):
+        forward(near, p)
+    for way in ways:
+        arrive_across(way, near, 0)
+    student_blocks(lambda i: (i - z > near) | (z - i > near))
+    stat[...] = jnp.zeros_like(stat)
+    softmax_part(s_exp, 0)
+
     per = width // tf
 
     def teacher_block(f):
@@ -423,10 +435,12 @@
 
     order = [*range(1, n_z), 0]
     hx, hz = {}, {}
-    rc = [to_mate(0, pm)]
+    rc = []
     for k in order:
         hx_out[k] = head_block(((z + k) % n_z) * COLS + px).astype(jnp.bfloat16)
         hx[k] = send(hx_out.at[k], hx_in.at[k], to_x)
+        if not rc:
+            rc.append(to_mate(0, pm))
     rc.append(to_mate(1, m))
     arrive(rc[0], rc_in.at[0])
     row_block(2 * g + pm, ry_out, rc_in.at[0])

time: 113 us -> 104 us (0.920)
  Pallas kernels: 108 us -> 98.8 us
    pallas_call x1, Pallas kernels: 108 us -> 98.8 us  [fused(): pl.pallas_call(functools.partial(step_kernel, n_dp), out_shape=(jax.Shape...]
where the time goes in v4:
time: 104 us
  Pallas kernels  98.8 us (95%)
  local copies, waits for them, and re-layouts  3.6 us (3%)
  between operations  1.29 us (1%)
    pallas_call x1, Pallas kernels, fused(): pl.pallas_call(functools.partial(step_kernel, n_dp), out_shape=(jax.Shape...  98.8 us
    unnamed x2, local copies, waits for them, and re-layouts  3.6 us

profile of v4, /device:TPU:0, one launch (start us, length us, event | category | flops | bytes accessed | tf_op | source)
XLA Modules:
  0.0 103.7 jit_solution(8336151679777645001)
XLA Ops:
  1.3 98.8 %shard_map.86 = (bf16[384,256]{1,0:T(8,128)(2,1)}, bf16[160,2048]{1,0:T(8,128)(2,1)}) custom-call(bf16[640,1280]{1,0:T(8,128)(2,1)} %t_rows.1, bf16[1280]{0:T(1024)(128)(2,1)} %t_gain.1, bf16[384,640]{1,0:T(8,128)(2,1)} %t_head.1, bf16[640,2048]{1,0:T(8,128)(2,1)} %s_rows.1, bf16[2048]{0:T(1024)(128)(2,1)} %s_gain.1, bf16[384,256]{1,0:T(8,128)(2,1)} %s_head.1, ...), custom_call_target="tpu_custom_call" | custom-call | tf_op jit(solution)/shard_map/pallas_call | solution.py:514
  100.1 1.6 %copy.12 = bf16[384,256]{1,0:T(8,128)(2,1)} copy(bf16[384,256]{1,0:T(8,128)(2,1)} %get-tuple-element.4) | data formatting | bytes 393216
  101.7 2.0 %copy.13 = bf16[160,2048]{1,0:T(8,128)(2,1)} copy(bf16[160,2048]{1,0:T(8,128)(2,1)} %get-tuple-element.5) | data formatting | bytes 1310720

commit v5 on v4

--- a/solution.py
+++ b/solution.py
@@ -112,10 +112,10 @@
 def step_kernel(
     n_dp,
     t_rows, t_gain, t_head, s_rows, s_gain, s_head, lengths,
-    head_out, row_out,
+    h_acc, r_acc, squares,
     rows_all, gain_all, ht, hs, srow, sn, tn, t_exp, s_exp, lg_t, lg,
-    stat, stat_in, hx_out, hx_in, hz_out, hz_in, h_acc,
-    rc_out, rc_in, ry_out, ry_in, r_acc, sq, sq_in, sq2, sq2_in,
+    stat, stat_in, hx_out, hx_in, hz_out, hz_in,
+    rc_out, rc_in, ry_out, ry_in, sq, sq_in, sq2, sq2_in,
     send_sem, recv_sem, local_sem,
 ):
     n_z = n_dp // COLS
@@ -410,7 +410,6 @@
 
     grad = s_exp[...] * factor(0) - t_exp[...] * factor(2)
     lg_t[...] = grad.astype(jnp.bfloat16)
-    lg[...] = grad.T.astype(jnp.bfloat16)
 
     def head_block(f):
         at = pl.ds(pl.multiple_of(f * sf, sf), sf)
@@ -429,21 +428,30 @@
 
         lax.fori_loop(0, n_dp, step, 0)
 
-    def to_mate(i, mp):
-        row_block(2 * pg + mp, rc_out.at[i])
-        return send(rc_out.at[i], rc_in.at[i], to_core)
+    def to_mate():
+        at = pl.ds(pl.multiple_of(2 * pg * own, own), 2 * own)
+
+        def step(f, _):
+            to = pl.ds(pl.multiple_of(f * sf, sf), sf)
+            value = jnp.dot(lg[at, :], hs[f], preferred_element_type=jnp.float32)
+            value = value.astype(jnp.bfloat16)
+            rc_out[0, :, to] = value[:own]
+            rc_out[1, :, to] = value[own:]
+            return 0
+
+        lax.fori_loop(0, n_dp, step, 0)
+        return [send(rc_out.at[mp], rc_in.at[mp], to_core) for mp in (pm, m)]
 
     order = [*range(1, n_z), 0]
     hx, hz = {}, {}
-    rc = []
     for k in order:
         hx_out[k] = head_block(((z + k) % n_z) * COLS + px).astype(jnp.bfloat16)
         hx[k] = send(hx_out.at[k], hx_in.at[k], to_x)
-        if not rc:
-            rc.append(to_mate(0, pm))
-    rc.append(to_mate(1, m))
-    arrive(rc[0], rc_in.at[0])
-    row_block(2 * g + pm, ry_out, rc_in.at[0])
+        if k == order[0]:
+            lg[...] = lg_t[...].T
+            rc = to_mate()
+    arrive(rc[0], rc_in.at[pm])
+    row_block(2 * g + pm, ry_out, rc_in.at[pm])
     ry = send(ry_out, ry_in, to_y)
     for k in order[:-1]:
         value = head_block(col(k))
@@ -453,8 +461,8 @@
     value = head_block(d)
     arrive(hx[0], hx_in.at[0])
     h_acc[...] = value + hx_in[0].astype(jnp.float32)
-    arrive(rc[1], rc_in.at[1])
-    row_block(2 * g + m, r_acc, rc_in.at[1])
+    arrive(rc[1], rc_in.at[m])
+    row_block(2 * g + m, r_acc, rc_in.at[m])
     for k in range(1, n_z):
         arrive(hz[k], hz_in.at[k - 1])
     total = h_acc[...] + sum(hz_in[k].astype(jnp.float32) for k in range(n_z - 1))
@@ -483,19 +491,19 @@
     second = [send(sq2, sq2_in.at[k - 1], {"dp": (d + k) % n_dp}) for k in range(1, n_dp)]
     for k in range(1, n_dp):
         arrive(second[k - 1], sq2_in.at[k - 1])
-    squares = jnp.sum(sq2[...] + jnp.sum(sq2_in[...], axis=0), axis=1, keepdims=True)
-    devices = n_dp * blocks
-    head_out[...] = (
-        h_acc[...] * lax.rsqrt(squares[0:1, :] / (voc * sf * devices) + epsilon)
-    ).astype(jnp.bfloat16)
-    row_out[...] = (
-        r_acc[...] * lax.rsqrt(squares[1:2, :] / (own * ds * devices) + epsilon)
-    ).astype(jnp.bfloat16)
+    squares[...] = sq2[...] + jnp.sum(sq2_in[...], axis=0)
     for copy, when in sent:
         if when is None:
             copy.wait_send()
         else:
             pl.when(when)(copy.wait_send)
+
+
+def scale_kernel(sizes, head_grad, row_grad, squares, head_update, row_update):
+    sums = jnp.sum(squares[...], axis=1, keepdims=True)
+    for i, (grad, update) in enumerate(((head_grad, head_update), (row_grad, row_update))):
+        scale = lax.rsqrt(sums[i : i + 1, :] / sizes[i] + epsilon)
+        update[...] = (grad[...] * scale).astype(jnp.bfloat16)
 
 
 def fused(
@@ -511,14 +519,15 @@
     copies = 3 + hops + 3 + 3 + 2 * n_z - 1 + 3 + 3 + n_dp - 1
     anywhere, vmem = pl.BlockSpec(memory_space=pl.ANY), pl.BlockSpec(memory_space=pltpu.VMEM)
     scalars = pl.BlockSpec(memory_space=pltpu.SMEM)
-    return pl.pallas_call(
+    grads = pl.pallas_call(
         functools.partial(step_kernel, n_dp),
         out_shape=(
-            jax.ShapeDtypeStruct((voc, sf), bf),
-            jax.ShapeDtypeStruct((own, ds), bf),
+            jax.ShapeDtypeStruct((voc, sf), f32),
+            jax.ShapeDtypeStruct((own, ds), f32),
+            jax.ShapeDtypeStruct((8, 128), f32),
         ),
         in_specs=[anywhere, vmem, anywhere, anywhere, vmem, anywhere, scalars],
-        out_specs=(vmem, vmem),
+        out_specs=(vmem, vmem, vmem),
         scratch_shapes=[
             pltpu.VMEM((4, tok, width), bf),
             pltpu.VMEM((4, 8, width), f32),
@@ -537,12 +546,10 @@
             pltpu.VMEM((n_z, voc, sf), bf),
             pltpu.VMEM((n_z - 1, voc, sf), bf),
             pltpu.VMEM((n_z - 1, voc, sf), bf),
-            pltpu.VMEM((voc, sf), f32),
             pltpu.VMEM((2, own, ds), bf),
             pltpu.VMEM((2, own, ds), bf),
             pltpu.VMEM((own, ds), bf),
             pltpu.VMEM((own, ds), bf),
-            pltpu.VMEM((own, ds), f32),
             pltpu.VMEM((8, 128), f32),
             pltpu.VMEM((3, 8, 128), f32),
             pltpu.VMEM((8, 128), f32),
@@ -563,6 +570,17 @@
         student_head,
         lengths,
     )
+    devices = 4 * n_dp
+    return pl.pallas_call(
+        functools.partial(scale_kernel, (voc * sf * devices, own * ds * devices)),
+        out_shape=(
+            jax.ShapeDtypeStruct((voc, sf), bf),
+            jax.ShapeDtypeStruct((own, ds), bf),
+        ),
+        in_specs=[vmem, vmem, vmem],
+        out_specs=(vmem, vmem),
+        compiler_params=pltpu.CompilerParams(vmem_limit_bytes=56 << 20),
+    )(*grads)
 
 
 def step(*args):

time: 104 us -> 103 us (level)
  local copies, waits for them, and re-layouts: 3.6 us -> 0 us
  Pallas kernels: 98.8 us -> 101 us
    unnamed x2 -> x0, local copies, waits for them, and re-layouts: 3.6 us -> none
    pallas_call x0 -> x1, Pallas kernels: none -> 2.48 us  [fused(): pl.pallas_call(functools.partial(scale_kernel, (voc * sf * devices, own *...]
where the time goes in v5:
time: 103 us
  Pallas kernels  101 us (98%)
  between operations  1.29 us (1%)
    pallas_call x1, Pallas kernels, fused(): pl.pallas_call(functools.partial(step_kernel, n_dp), out_shape=(jax.Shape...  99 us
    pallas_call x1, Pallas kernels, fused(): pl.pallas_call(functools.partial(scale_kernel, (voc * sf * devices, own *...  2.48 us

profile of v5, /device:TPU:0, one launch (start us, length us, event | category | flops | bytes accessed | tf_op | source)
XLA Modules:
  0.0 102.8 jit_solution(13071773262453487322)
XLA Ops:
  1.3 99.0 %shard_map.86 = (f32[384,256]{1,0:T(8,128)}, f32[160,2048]{1,0:T(8,128)}, f32[8,128]{1,0:T(8,128)}) custom-call(bf16[640,1280]{1,0:T(8,128)(2,1)} %t_rows.1, bf16[1280]{0:T(1024)(128)(2,1)} %t_gain.1, bf16[384,640]{1,0:T(8,128)(2,1)} %t_head.1, bf16[640,2048]{1,0:T(8,128)(2,1)} %s_rows.1, bf16[2048]{0:T(1024)(128)(2,1)} %s_gain.1, bf16[384,256]{1,0:T(8,128)(2,1)} %s_head.1, ...), custom_call_target="tpu_custom_call" | custom-call | tf_op jit(solution)/shard_map/pallas_call | solution.py:522
  100.3 2.5 %shard_map.87 = (bf16[384,256]{1,0:T(8,128)(2,1)}, bf16[160,2048]{1,0:T(8,128)(2,1)}) custom-call(f32[384,256]{1,0:T(8,128)} %get-tuple-element.5.head_grad, f32[160,2048]{1,0:T(8,128)} %get-tuple-element.6.row_grad, f32[8,128]{1,0:T(8,128)} %get-tuple-element.7.squares), custom_call_target="tpu_custom_call" | custom-call | tf_op jit(solution)/shard_map/pallas_call | solution.py:574

commit v6 on v5

--- a/solution.py
+++ b/solution.py
@@ -199,6 +199,8 @@
         return (at >= 0) & (at < n_z)
 
     along, across = {}, {}
+    halves = [pl.ds(h * (tok // 2), tok // 2) for h in range(2)]
+    rows_far = []
     for p, (src, dst, c) in enumerate(parts):
         for way in ways:
             along[way, 0, p] = send(
@@ -207,7 +209,7 @@
             )
         across[p] = send(view(src, c), view(dst.at[d], c), to_x)
         if p == 0:
-            rows_y = send(t_rows, rows_all.at[me], to_y)
+            rows_y = [send(t_rows.at[at, :], rows_all.at[me, at, :], to_y) for at in halves]
     rows_core = send(t_rows, rows_all.at[me], to_core)
     gains = [send(gain_all.at[me], gain_all.at[me], peer) for peer in peers]
 
@@ -325,8 +327,10 @@
             forward(hop, p)
             if hop == 0:
                 turn(p)
-    arrive(rows_y, rows_all.at[peers_gm[0]])
-    rows_far = send(rows_all.at[peers_gm[0]], rows_all.at[peers_gm[0]], to_core)
+        if hop < 2:
+            slot = rows_all.at[peers_gm[0], halves[hop], :]
+            arrive(rows_y[hop], slot)
+            rows_far.append(send(slot, slot, to_core))
 
     near = n_z - 2
     locals_[3].wait()
@@ -335,11 +339,15 @@
             arrive_across(way, hop, 0)
     s_exp[...] = jnp.zeros_like(s_exp)
     student_blocks(lambda i: (i - z <= near) & (z - i <= near))
+    bend_on(bent[0])
+    forward(near, 0)
+    forward(near, 1)
     locals_[1].wait()
     for i in range(3):
         arrive(gains[i], gain_all.at[peers_gm[i]])
     arrive(rows_core, rows_all.at[peers_gm[1]])
-    arrive(rows_far, rows_all.at[peers_gm[2]])
+    for h in range(2):
+        arrive(rows_far[h], rows_all.at[peers_gm[2], halves[h], :])
     width = t_rows.shape[1]
 
     def teacher_tile(i, _):
@@ -356,9 +364,8 @@
 
     lax.fori_loop(0, tok // tile, teacher_tile, 0)
 
+    bend_on(bent[1])
     for p in bent:
-        bend_on(p)
-    for p in range(len(parts)):
         forward(near, p)
     for way in ways:
         arrive_across(way, near, 0)
@@ -516,7 +523,7 @@
     n_z, own = n_dp // COLS, tok // 4
     bf, f32 = jnp.bfloat16, jnp.float32
     hops = (1 + CHUNKS) * ((n_z - 1) * 4 + 3)
-    copies = 3 + hops + 3 + 3 + 2 * n_z - 1 + 3 + 3 + n_dp - 1
+    copies = 5 + hops + 3 + 3 + 2 * n_z - 1 + 3 + 3 + n_dp - 1
     anywhere, vmem = pl.BlockSpec(memory_space=pl.ANY), pl.BlockSpec(memory_space=pltpu.VMEM)
     scalars = pl.BlockSpec(memory_space=pltpu.SMEM)
     grads = pl.pallas_call(

time: 103 us -> 104 us (level)
  no operation moved by 1% of the time
where the time goes in v6:
time: 104 us
  Pallas kernels  102 us (98%)
  between operations  1.29 us (1%)
    pallas_call x1, Pallas kernels, fused(): pl.pallas_call(functools.partial(step_kernel, n_dp), out_shape=(jax.Shape...  100 us
    pallas_call x1, Pallas kernels, fused(): pl.pallas_call(functools.partial(scale_kernel, (voc * sf * devices, own *...  2.48 us

profile of v6, /device:TPU:0, one launch (start us, length us, event | category | flops | bytes accessed | tf_op | source)
XLA Modules:
  0.0 103.8 jit_solution(4899660398248147853)
XLA Ops:
  1.3 100.0 %shard_map.86 = (f32[384,256]{1,0:T(8,128)}, f32[160,2048]{1,0:T(8,128)}, f32[8,128]{1,0:T(8,128)}) custom-call(bf16[640,1280]{1,0:T(8,128)(2,1)} %t_rows.1, bf16[1280]{0:T(1024)(128)(2,1)} %t_gain.1, bf16[384,640]{1,0:T(8,128)(2,1)} %t_head.1, bf16[640,2048]{1,0:T(8,128)(2,1)} %s_rows.1, bf16[2048]{0:T(1024)(128)(2,1)} %s_gain.1, bf16[384,256]{1,0:T(8,128)(2,1)} %s_head.1, ...), custom_call_target="tpu_custom_call" | custom-call | tf_op jit(solution)/shard_map/pallas_call | solution.py:529
  101.3 2.5 %shard_map.87 = (bf16[384,256]{1,0:T(8,128)(2,1)}, bf16[160,2048]{1,0:T(8,128)(2,1)}) custom-call(f32[384,256]{1,0:T(8,128)} %get-tuple-element.5.head_grad, f32[160,2048]{1,0:T(8,128)} %get-tuple-element.6.row_grad, f32[8,128]{1,0:T(8,128)} %get-tuple-element.7.squares), custom_call_target="tpu_custom_call" | custom-call | tf_op jit(solution)/shard_map/pallas_call | solution.py:581

commit v7 on v5

--- a/solution.py
+++ b/solution.py
@@ -358,38 +358,50 @@
 
     for p in bent:
         bend_on(p)
-    for p in range(len(parts)):
+    passed = [p for p in range(len(parts)) if p not in bent]
+    for p in passed:
         forward(near, p)
+
+    per = width // tf
+
+    def teacher_block(f):
+        at = pl.ds(pl.multiple_of((f % per) * tf, tf), tf)
+        t_exp[...] += dot_nt(ht[f], tn[f // per, :, at])
+
+    def teacher_column(which):
+        def step(i, _):
+            @pl.when(which(i))
+            def _():
+                teacher_block(i * COLS + x)
+
+            return 0
+
+        lax.fori_loop(0, n_z, step, 0)
+
+    def teacher_across(hop):
+        for way in ways:
+            for p in range(1, len(parts)):
+                arrive_across(way, hop, p)
+
+            @pl.when(inside(origin(way, hop)))
+            def _():
+                teacher_block(block(way, hop, px))
+
+    locals_[2].wait()
+    t_exp[...] = jnp.zeros_like(t_exp)
+    teacher_column(lambda i: (i - z <= near) & (z - i <= near))
+    teacher_block(z * COLS + px)
+    for hop in range(near):
+        teacher_across(hop)
     for way in ways:
         arrive_across(way, near, 0)
     student_blocks(lambda i: (i - z > near) | (z - i > near))
     stat[...] = jnp.zeros_like(stat)
     softmax_part(s_exp, 0)
-
-    per = width // tf
-
-    def teacher_block(f):
-        at = pl.ds(pl.multiple_of((f % per) * tf, tf), tf)
-        t_exp[...] += dot_nt(ht[f], tn[f // per, :, at])
-
-    locals_[2].wait()
-    t_exp[...] = jnp.zeros_like(t_exp)
-
-    def own_column(i, _):
-        teacher_block(i * COLS + x)
-        return 0
-
-    lax.fori_loop(0, n_z, own_column, 0)
-    teacher_block(z * COLS + px)
-    for hop in range(n_z - 1):
-        for way in ways:
-            for p in range(1, len(parts)):
-                arrive_across(way, hop, p)
-
-            @pl.when(inside(origin(way, hop)))
-            def _():
-                teacher_block(block(way, hop, px))
-
+    for p in bent:
+        forward(near, p)
+    teacher_column(lambda i: (i - z > near) | (z - i > near))
+    teacher_across(near)
     softmax_part(t_exp, 2)
 
     stats = [send(stat, stat_in.at[i], peers[i]) for i in range(3)]

time: 103 us -> 102 us (level)
  no operation moved by 1% of the time
where the time goes in v7:
time: 102 us
  Pallas kernels  101 us (99%)
  between operations  1.29 us (1%)
    pallas_call x1, Pallas kernels, fused(): pl.pallas_call(functools.partial(step_kernel, n_dp), out_shape=(jax.Shape...  98.1 us
    pallas_call x1, Pallas kernels, fused(): pl.pallas_call(functools.partial(scale_kernel, (voc * sf * devices, own *...  2.48 us

profile of v7, /device:TPU:0, one launch (start us, length us, event | category | flops | bytes accessed | tf_op | source)
XLA Modules:
  0.0 101.8 jit_solution(6102886599052566180)
XLA Ops:
  1.3 98.1 %shard_map.86 = (f32[384,256]{1,0:T(8,128)}, f32[160,2048]{1,0:T(8,128)}, f32[8,128]{1,0:T(8,128)}) custom-call(bf16[640,1280]{1,0:T(8,128)(2,1)} %t_rows.1, bf16[1280]{0:T(1024)(128)(2,1)} %t_gain.1, bf16[384,640]{1,0:T(8,128)(2,1)} %t_head.1, bf16[640,2048]{1,0:T(8,128)(2,1)} %s_rows.1, bf16[2048]{0:T(1024)(128)(2,1)} %s_gain.1, bf16[384,256]{1,0:T(8,128)(2,1)} %s_head.1, ...), custom_call_target="tpu_custom_call" | custom-call | tf_op jit(solution)/shard_map/pallas_call | solution.py:534
  99.3 2.5 %shard_map.87 = (bf16[384,256]{1,0:T(8,128)(2,1)}, bf16[160,2048]{1,0:T(8,128)(2,1)}) custom-call(f32[384,256]{1,0:T(8,128)} %get-tuple-element.5.head_grad, f32[160,2048]{1,0:T(8,128)} %get-tuple-element.6.row_grad, f32[8,128]{1,0:T(8,128)} %get-tuple-element.7.squares), custom_call_target="tpu_custom_call" | custom-call | tf_op jit(solution)/shard_map/pallas_call | solution.py:586
